TPU v7x, 32 devices: a whole 2x2x4 slice. The times are simulated.
32 devices in a mesh: roll: 16 (over z, x, core), seq: 2 (over y).
Axes of the slice: x: 2, y: 2, z: 4, core: 2. Of those that a mesh axis runs over, the one named last changes fastest.
Arguments:
- hidden: bfloat16 [16, 1024, 2880], P('roll', 'seq'), may hold values from -6 to 6
- key_value_blocks: bfloat16 [2880, 1024], P('roll'), may hold values from -0.109375 to 0.109375
- block_of: int32 [16], replicated, may hold values from 0 to 15, each once
- queries: bfloat16 [16, 64, 4096], P('roll', 'seq'), may hold values from -480 to 480
- key_pos: int32 [16, 1024], P('roll', 'seq'), may hold values from 0 to 5118, as said below
- query_pos: int32 [16, 64], P('roll', 'seq'), may hold values from 0 to 5118, as said below
Outputs:
- context: bfloat16 [16, 64, 4096], P('roll', 'seq')
Inputs may be any that keep to these rules, and one draw needn't show every extreme that they name: Along each sequence key_pos rises by one from that sequence's start; starts lie in 0 to 4095 and some sequence starts at 0, another at 4095. `query_pos`: each query position lies between the first and the last key position of its sequence.
All inputs are finite; a program needn't handle non-finite values.
Results may differ from a plain program's by a relative error of at most 0.017.
The roundings to bfloat16 on the way count: a program that leaves them out, or rounds other values in their place, can miss the bound.
Values may be sent and summed in bfloat16 or wider, within the bound.
A program may use at most 64 MiB of HBM per device.

v0:
```python
import math

import jax
import jax.numpy as jnp
from jax import lax
from jax.sharding import PartitionSpec as P

QUERY_HEAD_COUNT = 64
HEAD_WIDTH = 64


rope_base = 150000.0


def rotary(vectors, positions):
    head_size = vectors.shape[-1]
    half = head_size // 2
    freq = rope_base ** (-(jnp.arange(half).astype(jnp.float32) * 2.0 / head_size))
    angle = positions.astype(jnp.float32)[:, None] * freq[None, :]
    cosine = jnp.cos(angle)[:, None, :]
    sine = jnp.sin(angle)[:, None, :]
    first = vectors[..., :half]
    second = vectors[..., half:]
    return jnp.concatenate(
        [first * cosine - second * sine, second * cosine + first * sine], axis=-1
    )


def shards(hidden, key_value_blocks, block_of, queries, key_pos, query_pos):
    local_rows = hidden[0]
    row_count = local_rows.shape[0]
    block_rows = key_value_blocks.shape[0]
    all_columns = key_value_blocks.shape[1]
    seq_devices = lax.axis_size("seq")
    kv_heads_all = all_columns // (2 * HEAD_WIDTH)
    local_heads = kv_heads_all // seq_devices
    query_group = QUERY_HEAD_COUNT // kv_heads_all
    query_local = queries[0]
    query_count = query_local.shape[0]
    rotated_rows = rotary(
        query_local.astype(jnp.float32).reshape(query_count, QUERY_HEAD_COUNT, HEAD_WIDTH),
        query_pos[0],
    )
    rotated_rows = rotated_rows.astype(jnp.bfloat16).reshape(
        query_count, kv_heads_all, query_group * HEAD_WIDTH
    )
    piece = lax.all_gather(key_value_blocks, "roll", axis=0, tiled=True)
    count = piece.shape[0] // block_rows

    def one_block(offset, accum):
        logical = block_of[offset]
        hidden_cols = lax.dynamic_slice_in_dim(local_rows, logical * block_rows, block_rows, 1)
        weight_rows = lax.dynamic_slice_in_dim(piece, offset * block_rows, block_rows, 0)
        return accum + jnp.dot(hidden_cols, weight_rows, preferred_element_type=jnp.float32)

    projected_rows = lax.fori_loop(
        0, count, one_block, jnp.zeros((row_count, all_columns), jnp.float32)
    )
    projected_rows = projected_rows.reshape(row_count, kv_heads_all, 2 * HEAD_WIDTH)
    keys = rotary(projected_rows[..., :HEAD_WIDTH], key_pos[0]).astype(jnp.bfloat16)
    values = projected_rows[..., HEAD_WIDTH:].astype(jnp.bfloat16)
    packed = jnp.concatenate([keys, values], axis=-1)
    kv_local, query_heads = (
        lax.all_to_all(packed, "seq", split_axis=1, concat_axis=0, tiled=True),
        lax.all_to_all(rotated_rows, "seq", split_axis=1, concat_axis=0, tiled=True),
    )
    all_key_pos, all_query_pos = (
        lax.all_gather(key_pos[0], "seq", axis=0, tiled=True),
        lax.all_gather(query_pos[0], "seq", axis=0, tiled=True),
    )
    total_queries = query_heads.shape[0]
    block_queries = math.gcd(total_queries, 64)
    block_count = total_queries // block_queries
    scale = 1.0 / jnp.sqrt(jnp.float32(HEAD_WIDTH))

    def attend(index):
        head = index // block_count
        block = index % block_count
        query_block = lax.dynamic_slice(
            query_heads,
            (block * block_queries, head, 0),
            (block_queries, 1, query_group * HEAD_WIDTH),
        )
        query_block = query_block.reshape(block_queries * query_group, HEAD_WIDTH)
        head_kv = lax.dynamic_index_in_dim(kv_local, head, 1, False)
        positions = lax.dynamic_slice_in_dim(all_query_pos, block * block_queries, block_queries)
        row_pos = jnp.repeat(positions, query_group)
        scores = (
            lax.dot_general(
                query_block,
                head_kv[:, :HEAD_WIDTH],
                (((1,), (1,)), ((), ())),
                preferred_element_type=jnp.float32,
            )
            * scale
        )
        allowed = all_key_pos[None, :] <= row_pos[:, None]
        scores = jnp.where(allowed, scores, -1e30)
        top = jnp.max(scores, axis=1, keepdims=True)
        expo = jnp.where(allowed, jnp.exp(scores - top), 0.0)
        probs = (expo / jnp.sum(expo, axis=1, keepdims=True)).astype(jnp.bfloat16)
        result = jnp.dot(probs, head_kv[:, HEAD_WIDTH:], preferred_element_type=jnp.float32).astype(
            jnp.bfloat16
        )
        return result.reshape(block_queries, query_group * HEAD_WIDTH)

    outputs = lax.map(attend, jnp.arange(local_heads * block_count))
    outputs = outputs.reshape(
        local_heads, block_count, block_queries, query_group * HEAD_WIDTH
    ).transpose(1, 2, 0, 3)
    outputs = outputs.reshape(total_queries, local_heads, query_group * HEAD_WIDTH)
    returned = lax.all_to_all(outputs, "seq", split_axis=0, concat_axis=1, tiled=True)
    return returned.reshape(1, query_count, QUERY_HEAD_COUNT * HEAD_WIDTH)


def solution(mesh):
    return jax.shard_map(
        shards,
        mesh=mesh,
        in_specs=(
            P("roll", "seq", None),
            P("roll", None),
            P(),
            P("roll", "seq", None),
            P("roll", "seq"),
            P("roll", "seq"),
        ),
        out_specs=P("roll", "seq", None),
        check_vma=False,
    )
```

profile of v0, /device:TPU:0, one launch (start us, length us, event | category | flops | bytes accessed | tf_op | source)
XLA Modules:
  0.0 198.8 jit_solution(9774860951773870918)
XLA Ops:
  6.5 0.7 all-gather.5.cloned.1.call-update
  7.3 1.4 reshape.150
  8.6 0.7 convert_bitcast_fusion
  10.6 0.8 copy.28
  11.4 4.2 %all-to-all-start = ((bf16[32,8,512]{2,0,1:T(8,128)(2,1)}), bf16[32,8,512]{2,0,1:T(8,128)(2,1)S(1)}, u32[]{:S(2)}, u32[]{:S(2)}) async-start(bf16[32,8,512]{2,0,1:T(8,128)(2,1)} %copy.28), calls=%async_computation | async-start | bytes 524288 | tf_op jit(solution)/shard_map/all_to_all | solution.py:65
  15.6 4.6 %copy.30 = bf16[1,512,2880]{2,1,0:T(8,128)(2,1)} copy(bf16[1,512,2880]{1,2,0:T(8,128)(2,1)} %param.10) | data formatting | bytes 5898240 | tf_op args[0]
  20.6 52.3 %all-gather.5.cloned.1.call-done = bf16[16,180,1024]{2,1,0:T(8,128)(2,1)} async-done(((bf16[1,180,1024]{2,1,0:T(8,128)(2,1)}), bf16[16,180,1024]{2,1,0:T(8,128)(2,1)}) %all-gather.5.cloned.1.call-update) | async-done | bytes 5898256 | tf_op jit(solution)/shard_map/all_gather | solution.py:47
  72.8 8.0 %reshape.159 = bf16[2880,1024]{1,0:T(8,128)(2,1)} reshape(bf16[16,180,1024]{2,1,0:T(8,128)(2,1)} %all-gather.5.cloned.1.call-done) | data formatting | bytes 11796480
  80.8 52.2 %while.27 = (s32[]{:T(128)}, f32[512,1024]{1,0:T(8,128)S(1)}, s32[16]{0:T(128)S(1)}, bf16[512,2880]{1,0:T(8,128)(2,1)}, bf16[2880,1024]{1,0:T(8,128)(2,1)}, /*in...) while((s32[]{:T(128)}, f32[512,1024]{1,0:T(8,128)S(1)}, s32[16]{0:T(128)S(1)}, ...), condition=%wide.region_1.0_spmd.clone, body=%wide.region_0.0_spmd.clone.sunk | while | flops 189792272 | bytes 4833503 | solution.py:56
  82.1 2.0 select_add_fusion.2
  84.1 0.6 dynamic_slice.63
  85.4 2.0 select_add_fusion.2
  87.4 0.6 dynamic_slice.63
  88.6 2.0 select_add_fusion.2
  90.6 0.6 dynamic_slice.63
  91.9 2.0 select_add_fusion.2
  93.9 0.6 dynamic_slice.63
  95.2 2.0 select_add_fusion.2
  98.4 2.0 select_add_fusion.2
  101.7 2.0 select_add_fusion.2
  103.7 0.6 dynamic_slice.63
  105.0 2.0 select_add_fusion.2
  108.2 2.0 select_add_fusion.2
  111.5 2.0 select_add_fusion.2
  114.8 2.0 select_add_fusion.2
  118.0 2.0 select_add_fusion.2
  121.3 2.0 select_add_fusion.2
  124.6 1.9 select_add_fusion.2
  127.8 2.0 select_add_fusion.2
  131.1 2.0 select_add_fusion.2
  133.0 1.9 copy.31
  134.9 1.3 slice.56
  136.2 1.4 subtract_convert_fusion.1
  137.7 1.3 copy.32
  139.0 3.6 %all-to-all-start.1 = ((bf16[512,8,128]{2,0,1:T(8,128)(2,1)}), bf16[512,8,128]{2,0,1:T(8,128)(2,1)S(1)}, u32[]{:S(2)}, u32[]{:S(2)}) async-start(bf16[512,8,128]{2,0,1:T(8,128)(2,1)} %copy.32), calls=%async_computation.1 | async-start | bytes 2097152 | tf_op jit(solution)/shard_map/all_to_all | solution.py:64
  143.9 13.0 %all-reduce = s32[64]{0:T(128)S(1)} all-reduce(s32[64]{0:T(128)S(1)} %bitcast_dynamic-update-slice_fusion), channel_id=3, replica_groups=mesh['roll'=16,'seq'=2] {'seq'}, use_global_device_ids=true, to_apply=%add | all-reduce | flops 64 | bytes 512 | tf_op jit(solution)/shard_map/all_gather | solution.py:69
  157.0 4.3 %all-gather = s32[1,1024]{1,0:T(1,128)S(1)} all-gather(s32[1,512]{1,0:T(1,128)S(1)} %copy-done), channel_id=2, replica_groups=mesh['roll'=16,'seq'=2] {'seq'}, dimensions={1}, use_global_device_ids=true | all-gather | bytes 6144 | tf_op jit(solution)/shard_map/all_gather | solution.py:68
  161.4 21.8 %while.26 = (s32[]{:T(128)}, bf16[4,64,512]{2,1,0:T(8,128)(2,1)S(1)}, s32[1024]{0:T(1024)S(1)}, s32[64]{0:T(128)S(1)}, s32[4]{0:T(128)S(1)}, /*index=5*/bf16[64,...) while((s32[]{:T(128)}, bf16[4,64,512]{2,1,0:T(8,128)(2,1)S(1)}, ...), condition=%wide.region_5.6_spmd, body=%wide.region_2.5_spmd.sunk | while | flops 143162368 | bytes 8161695 | solution.py:107
  164.8 0.7 fusion.21
  165.5 1.0 convolution_convert_fusion.2
  170.3 0.7 fusion.21
  171.0 1.0 convolution_convert_fusion.2
  175.7 0.7 fusion.21
  176.4 1.0 convolution_convert_fusion.2
  181.2 0.7 fusion.21
  181.9 1.0 convolution_convert_fusion.2
  183.4 7.6 %all_to_all.51 = bf16[64,4,512]{2,1,0:T(4,128)(2,1)S(1)} all-to-all(bf16[64,4,512]{2,1,0:T(4,128)(2,1)S(1)} %bitcast.50), channel_id=1, replica_groups=mesh['roll'=16,'seq'=2] {'seq'}, dimensions={0} | all-to-all | bytes 524288 | tf_op jit(solution)/shard_map/all_to_all | solution.py:112
  191.0 0.9 reshape.149
  (80 shorter events, 17.0 us)
Async XLA Ops:
  6.5 66.3 %all-gather.5.cloned.1.call-start = ((), (), s32[]{:S(2)}) async-start(), calls=%async_computation.3 | async-start | bytes 6406144 | tf_op jit(solution)/shard_map/all_gather | solution.py:47
  10.0 5.7 %copy-start = (s32[1,512]{1,0:T(1,128)S(1)}, s32[1,512]{1,0:T(1,128)}, u32[]{:S(2)}) copy-start(s32[1,512]{1,0:T(1,128)} %param.14) | copy-start | bytes 6148
  11.4 127.6 %all-to-all-start = ((bf16[32,8,512]{2,0,1:T(8,128)(2,1)}), bf16[32,8,512]{2,0,1:T(8,128)(2,1)S(1)}, u32[]{:S(2)}, u32[]{:S(2)}) async-start(bf16[32,8,512]{2,0,1:T(8,128)(2,1)} %copy.28), calls=%async_computation | async-start | bytes 524288 | tf_op jit(solution)/shard_map/all_to_all | solution.py:65
  20.5 60.3 %copy-start.1 = (s32[16]{0:T(128)S(1)}, s32[16]{0:T(128)}, u32[]{:S(2)}) copy-start(s32[16]{0:T(128)} %param.12) | copy-start | bytes 196
  137.7 4.9 %copy-start.3 = (u32[32]{0:T(128)S(1)}, u32[32]{0:T(128)}, u32[]{:S(2)}) copy-start(u32[32]{0:T(128)} %constant.126) | copy-start | bytes 388
  137.7 6.2 %copy-start.2 = (s32[1,32]{1,0:T(1,128)S(1)}, s32[1,32]{1,0:T(1,128)}, u32[]{:S(2)}) copy-start(s32[1,32]{1,0:T(1,128)} %param.15) | copy-start | bytes 388
  139.0 22.3 %all-to-all-start.1 = ((bf16[512,8,128]{2,0,1:T(8,128)(2,1)}), bf16[512,8,128]{2,0,1:T(8,128)(2,1)S(1)}, u32[]{:S(2)}, u32[]{:S(2)}) async-start(bf16[512,8,128]{2,0,1:T(8,128)(2,1)} %copy.32), calls=%async_computation.1 | async-start | bytes 2097152 | tf_op jit(solution)/shard_map/all_to_all | solution.py:64
Sparse Core Ops, SparseCore 0:
  9.6 63.1 all-gather.4
where the time goes:
time: 200 us; the launch traced here: 199 us
  waiting for transfers between devices  53 us (26%)
  matrix products  37.5 us (19%)
  local copies, waits for them, and re-layouts  36.7 us (18%)
  blocking collectives  24.9 us (12%)
  loops' own time  18.5 us (9%)
  between operations  14.2 us (7%)
  starting transfers between devices  7.82 us (4%)
  other arithmetic  6.19 us (3%)
    all_gather x1, waiting for transfers between devices, shards(): piece = lax.all_gather(key_value_blocks, 'roll', axis=0, tiled=True)  52.3 us
    dot_general x16, matrix products, one_block(): jnp.dot(hidden_cols, weight_rows, preferred_element_type=jnp.float32)  31.3 us
    unnamed x13, local copies, waits for them, and re-layouts  13.3 us
    all_gather x1, blocking collectives, shards(): lax.all_gather(query_pos[0], 'seq', axis=0, tiled=True)  13 us
    another operation x1, loops' own time, shards(): lax.fori_loop(0, count, one_block, jnp.zeros((row_count, all_columns), jn...  10.7 us
    dynamic_slice x16, local copies, waits for them, and re-layouts, one_block(): logical = block_of[offset]  10.2 us
    another operation x1, loops' own time, shards(): outputs = lax.map(attend, jnp.arange(local_heads * block_count))  7.76 us
    all_to_all x1, blocking collectives, shards(): lax.all_to_all(outputs, 'seq', split_axis=0, concat_axis=1, tiled=True)  7.56 us
  transfers between devices with their start and end apart: 3, of which 1 were waited for; matrix products, arithmetic and copies ran while one was open for 33% of the time, Pallas kernels for 0%

commit v1 on v0

v1 whole, which is shorter than its diff:
```python
import functools

import jax
import jax.numpy as jnp
import numpy as np
from jax import lax
from jax.experimental import pallas as pl
from jax.experimental.pallas import tpu as pltpu
from jax.sharding import PartitionSpec as P

HEAD_WIDTH = 64
MESH = pl.DeviceIdType.MESH
MASKED = -1e30
rope_base = 150000.0


def kernel(
    n_roll,
    n_seq,
    block_of,
    w_ref,
    hidden_ref,
    q_ref,
    key_pos_ref,
    query_pos_ref,
    freq_col_ref,
    freq_row_ref,
    out_ref,
    w_all,
    hidden_vm,
    h_blocks,
    acc,
    cos_k,
    sin_k,
    kk,
    vv,
    q_all,
    qpos_all,
    o_send,
    o_recv,
    l_send,
    l_recv,
    o_own,
    l_own,
    hidden_sem,
    ring_send,
    ring_recv,
    sib_send,
    sib_recv,
    q_send_sem,
    q_recv_sem,
    qp_send_sem,
    qp_recv_sem,
    o_send_sem,
    o_recv_sem,
    l_send_sem,
    l_recv_sem,
):
    depth, columns = w_ref.shape
    rows = hidden_vm.shape[0]
    q_rows, q_width = q_ref.shape
    heads = columns // (2 * HEAD_WIDTH)
    group = q_width // HEAD_WIDTH // heads
    group_width = group * HEAD_WIDTH
    ring = n_roll // 2
    half_ring = ring // 2
    phases = 2
    width = columns // phases
    heads_per_phase = heads // phases

    me = lax.axis_index("roll")
    seq = lax.axis_index("seq")
    core = me % 2
    chip = me // 2
    along = chip // 2
    side = chip % 2
    place = along * (1 - side) + (ring - 1 - along) * side

    def roll_of(position, which_core):
        position = (position + 2 * ring) % ring
        high = position // half_ring
        where = (1 - high) * (2 * position) + high * (2 * (ring - 1 - position) + 1)
        return 2 * where + which_core

    right = roll_of(place + 1, core)
    left = roll_of(place - 1, core)
    sibling = 2 * chip + 1 - core

    barrier = pltpu.get_barrier_semaphore()
    for other in (left, right, sibling):
        pl.semaphore_signal(barrier, inc=1, device_id=(other, seq), device_id_type=MESH)
    for i in range(1, n_seq):
        pl.semaphore_signal(
            barrier, inc=1, device_id=(me, (seq + i) % n_seq), device_id_type=MESH
        )
    pl.semaphore_wait(barrier, 3 + n_seq - 1)

    hidden_copy = pltpu.make_async_copy(hidden_ref, hidden_vm, hidden_sem)
    hidden_copy.start()

    def cols(phase, part):
        if part is None:
            return pl.ds(phase * width, width)
        return pl.ds(phase * width + part * (width // 2), width // 2)

    def ring_copy(phase, direction, step, part, own=False):
        origin = roll_of(place - (step - 1) * (1 - 2 * direction), core)
        c = cols(phase, part)
        return pltpu.make_async_remote_copy(
            src_ref=w_ref.at[:, c] if own else w_all.at[origin, :, c],
            dst_ref=w_all.at[origin, :, c],
            send_sem=ring_send.at[phase, direction, step - 1],
            recv_sem=ring_recv.at[phase, direction, step - 1],
            device_id=(right if direction == 0 else left, seq),
            device_id_type=MESH,
        )

    def ring_arrival(phase, direction, step, part):
        origin = roll_of(place - step * (1 - 2 * direction), core)
        c = cols(phase, part)
        return pltpu.make_async_remote_copy(
            src_ref=w_all.at[origin, :, c],
            dst_ref=w_all.at[origin, :, c],
            send_sem=ring_send.at[phase, direction, step - 1],
            recv_sem=ring_recv.at[phase, direction, step - 1],
            device_id=(right if direction == 0 else left, seq),
            device_id_type=MESH,
        )

    def sib_copy(phase, direction, step, part, which_core, own=False):
        origin = roll_of(place - step * (1 - 2 * direction), which_core)
        c = cols(phase, part)
        return pltpu.make_async_remote_copy(
            src_ref=w_ref.at[:, c] if own else w_all.at[origin, :, c],
            dst_ref=w_all.at[origin, :, c],
            send_sem=sib_send.at[phase, direction, step],
            recv_sem=sib_recv.at[phase, direction, step],
            device_id=(sibling, seq),
            device_id_type=MESH,
        )

    def start_phase(phase):
        for direction in range(2):
            ring_copy(phase, direction, 1, None if half_ring > 1 else direction, own=True).start()
        sib_copy(phase, 0, 0, None, core, own=True).start()

    start_phase(0)

    lane = lax.broadcasted_iota(jnp.int32, (q_rows, 128), 1)
    on_diag = lax.broadcasted_iota(jnp.int32, (q_rows, q_rows), 0) == lax.broadcasted_iota(
        jnp.int32, (q_rows, q_rows), 1
    )
    q_pos_row = query_pos_ref[...].astype(jnp.float32)
    q_pos_col = jnp.sum(
        jnp.where(on_diag, jnp.broadcast_to(q_pos_row, (q_rows, q_rows)), 0.0),
        axis=1,
        keepdims=True,
    )
    qpos_all[seq] = jnp.broadcast_to(q_pos_col, (q_rows, 128))
    q_angle = q_pos_col * freq_row_ref[...]
    q_cos = jnp.cos(q_angle)
    q_sin = jnp.sin(q_angle)
    first_half = lane % HEAD_WIDTH < HEAD_WIDTH // 2
    q_sin = jnp.where(first_half, -q_sin, q_sin)
    scale = HEAD_WIDTH ** -0.5
    for t in range(q_width // 128):
        x = q_ref[:, t * 128 : (t + 1) * 128].astype(jnp.float32)
        swapped = jnp.where(
            first_half,
            pltpu.roll(x, 128 - HEAD_WIDTH // 2, 1),
            pltpu.roll(x, HEAD_WIDTH // 2, 1),
        )
        rotated = (x * q_cos + swapped * q_sin).astype(jnp.bfloat16)
        q_all[seq, :, t * 128 : (t + 1) * 128] = (
            rotated.astype(jnp.float32) * scale
        ).astype(jnp.bfloat16)

    def q_copies(i, origin):
        target = (me, (seq + i) % n_seq)
        return (
            pltpu.make_async_remote_copy(
                src_ref=q_all.at[origin],
                dst_ref=q_all.at[origin],
                send_sem=q_send_sem.at[i],
                recv_sem=q_recv_sem.at[i],
                device_id=target,
                device_id_type=MESH,
            ),
            pltpu.make_async_remote_copy(
                src_ref=qpos_all.at[origin],
                dst_ref=qpos_all.at[origin],
                send_sem=qp_send_sem.at[i],
                recv_sem=qp_recv_sem.at[i],
                device_id=target,
                device_id_type=MESH,
            ),
        )

    for i in range(1, n_seq):
        for copy in q_copies(i, seq):
            copy.start()

    k_pos = key_pos_ref[...].astype(jnp.float32)
    k_angle = freq_col_ref[...] * k_pos
    cos_k[...] = jnp.cos(k_angle)
    sin_k[...] = jnp.sin(k_angle)

    hidden_copy.wait()
    for b in range(n_roll):
        h_blocks[b] = hidden_vm[:, b * depth : (b + 1) * depth]

    def multiply(block, phase, own=False, first=False):
        logical = block_of[block]
        c = cols(phase, None)
        weights = w_ref[:, c] if own else w_all[block, :, c]
        product = jnp.dot(h_blocks[logical], weights, preferred_element_type=jnp.float32)
        if first:
            acc[:, c] = product
        else:
            acc[:, c] += product

    for phase in range(phases):
        multiply(me, phase, own=True, first=True)

        def step_body(step, carry):
            for direction in range(2):
                ring_arrival(phase, direction, step, None).wait_recv()

                if half_ring > 2:

                    @pl.when(step < half_ring - 1)
                    def _():
                        ring_copy(phase, direction, step + 1, None).start()

                @pl.when(step == half_ring - 1)
                def _():
                    ring_copy(phase, direction, step + 1, direction).start()

                sib_copy(phase, direction, step, None, core).start()
            multiply(roll_of(place - step, core), phase)
            multiply(roll_of(place + step, core), phase)

            @pl.when(step == 1)
            def _():
                sib_copy(phase, 0, 0, None, 1 - core).wait_recv()
                multiply(sibling, phase)

            @pl.when(step > 1)
            def _():
                for direction in range(2):
                    sib_copy(phase, direction, step - 1, None, 1 - core).wait_recv()
                    multiply(
                        roll_of(place - (step - 1) * (1 - 2 * direction), 1 - core), phase
                    )

            return carry

        lax.fori_loop(1, half_ring, step_body, 0)
        if phase + 1 < phases:
            start_phase(phase + 1)
        for direction in range(2):
            ring_arrival(phase, direction, half_ring, direction).wait_recv()
            sib_copy(phase, direction, half_ring, direction, core).start()
        for direction in range(2):
            sib_copy(phase, direction, half_ring - 1, None, 1 - core).wait_recv()
            multiply(
                roll_of(place - (half_ring - 1) * (1 - 2 * direction), 1 - core), phase
            )
        multiply(roll_of(place + half_ring, core), phase)
        for direction in range(2):
            sib_copy(phase, direction, half_ring, direction, 1 - core).wait_recv()
        multiply(roll_of(place + half_ring, 1 - core), phase)

    lane_k = lax.broadcasted_iota(jnp.int32, (rows, 128), 1)
    cos_keys = cos_k[...]
    sin_keys = sin_k[...]

    def prepare(h, carry):
        both = acc[:, pl.ds(pl.multiple_of(h * 128, 128), 128)]
        turned = both.T
        first = turned[: HEAD_WIDTH // 2]
        second = turned[HEAD_WIDTH // 2 : HEAD_WIDTH]
        key = jnp.concatenate(
            [first * cos_keys - second * sin_keys, second * cos_keys + first * sin_keys], axis=0
        )
        kk[h] = jnp.concatenate([key, key], axis=0).astype(jnp.bfloat16)
        value = jnp.where(lane_k < HEAD_WIDTH, pltpu.roll(both, HEAD_WIDTH, 1), both)
        vv[h] = jnp.concatenate([value, jnp.ones_like(value)], axis=1).astype(jnp.bfloat16)
        return carry

    lax.fori_loop(0, heads, prepare, 0)

    def o_copy(i, h):
        c = pl.ds(pl.multiple_of(h * group_width, group_width), group_width)
        return pltpu.make_async_remote_copy(
            src_ref=o_send.at[i, :, c],
            dst_ref=o_recv.at[i, :, c],
            send_sem=o_send_sem.at[i, h],
            recv_sem=o_recv_sem.at[i, h],
            device_id=(me, (seq + i) % n_seq),
            device_id_type=MESH,
        )

    def l_copy(i):
        return pltpu.make_async_remote_copy(
            src_ref=l_send.at[i],
            dst_ref=l_recv.at[i],
            send_sem=l_send_sem.at[i],
            recv_sem=l_recv_sem.at[i],
            device_id=(me, (seq + i) % n_seq),
            device_id_type=MESH,
        )

    left_lanes = lane < HEAD_WIDTH
    pairs = group // 2

    def attend(i, h, allowed, packed):
        target = (seq + i) % n_seq
        base = pl.multiple_of(h * group_width, group_width)
        queries = q_all[target, :, pl.ds(base, group_width)]
        parts = []
        for j in range(pairs):
            two = queries[:, j * 128 : (j + 1) * 128]
            parts.append(jnp.where(left_lanes, two, jnp.zeros_like(two)))
            parts.append(jnp.where(left_lanes, jnp.zeros_like(two), two))
        stacked = jnp.concatenate(parts, axis=0)
        scores = jnp.dot(stacked, kk[h], preferred_element_type=jnp.float32)
        scores = scores.reshape(group, q_rows, rows)
        scores = jnp.where(allowed[None], scores, MASKED).reshape(group * q_rows, rows)
        top = jnp.max(scores, axis=1, keepdims=True)
        probs = jnp.exp(scores - top).astype(jnp.bfloat16)
        result = jnp.dot(probs, vv[h], preferred_element_type=jnp.float32)
        total = result[:, 128:]
        normal = result[:, :128] / total
        logs = top + jnp.log(total)
        for j in range(pairs):
            even = slice(2 * j * q_rows, (2 * j + 1) * q_rows)
            odd = slice((2 * j + 1) * q_rows, (2 * j + 2) * q_rows)
            tile = jnp.where(left_lanes, normal[even], normal[odd])
            c = pl.ds(pl.multiple_of(base + j * 128, 128), 128)
            if i == 0:
                o_own[:, c] = tile
            else:
                o_send[i, :, c] = tile.astype(jnp.bfloat16)
            packed = jnp.where(lane == h * group + 2 * j, logs[even], packed)
            packed = jnp.where(lane == h * group + 2 * j + 1, logs[odd], packed)
        return packed

    for i in list(range(1, n_seq)) + [0]:
        if i:
            for copy in q_copies(i, (seq - i + n_seq) % n_seq):
                copy.wait_recv()

    for i in list(range(1, n_seq)) + [0]:
        target = (seq + i) % n_seq
        allowed = k_pos <= qpos_all[target][:, 0:1]

        def one_head(h, packed):
            packed = attend(i, h, allowed, packed)
            if i:
                o_copy(i, h).start()
            return packed

        packed = lax.fori_loop(0, heads, one_head, jnp.zeros((q_rows, 128), jnp.float32))
        if i:
            l_send[i] = packed
            l_copy(i).start()
        else:
            l_own[...] = packed

    for i in range(1, n_seq):
        l_copy(i).wait_recv()

        def wait_head(h, carry):
            o_copy(i, h).wait_recv()
            return carry

        lax.fori_loop(0, heads, wait_head, 0)

    logs = [l_own[...]] + [l_recv[i] for i in range(1, n_seq)]
    top = functools.reduce(jnp.maximum, logs)
    shares = [jnp.exp(entry - top) for entry in logs]
    whole = functools.reduce(jnp.add, shares)
    shares = [entry / whole for entry in shares]
    for t in range(q_width // 128):
        c = slice(t * 128, (t + 1) * 128)
        total = None
        for i in range(n_seq):
            share = jnp.where(
                left_lanes, shares[i][:, 2 * t : 2 * t + 1], shares[i][:, 2 * t + 1 : 2 * t + 2]
            )
            part = o_own[:, c] if i == 0 else o_recv[i, :, c].astype(jnp.float32)
            total = share * part if total is None else total + share * part
        out_ref[:, c] = total.astype(jnp.bfloat16)

    for i in range(1, n_seq):
        for copy in q_copies(i, seq):
            copy.wait_send()
        l_copy(i).wait_send()

        def sent_head(h, carry):
            o_copy(i, h).wait_send()
            return carry

        lax.fori_loop(0, heads, sent_head, 0)
    for phase in range(phases):
        sib_copy(phase, 0, 0, None, core, own=True).wait_send()

        def sent_step(step, carry):
            for direction in range(2):
                ring_copy(phase, direction, step, None).wait_send()
                sib_copy(phase, direction, step, None, core).wait_send()
            return carry

        lax.fori_loop(1, half_ring, sent_step, 0)
        for direction in range(2):
            ring_copy(phase, direction, half_ring, direction).wait_send()
            sib_copy(phase, direction, half_ring, direction, core).wait_send()


def shards(n_roll, n_seq, hidden, key_value_blocks, block_of, queries, key_pos, query_pos):
    rows, model_width = hidden.shape[1:]
    depth, columns = key_value_blocks.shape
    q_rows, q_width = queries.shape[1:]
    heads = columns // (2 * HEAD_WIDTH)
    half = HEAD_WIDTH // 2
    freq = rope_base ** (-(np.arange(half) * 2.0 / HEAD_WIDTH))
    freq = freq.astype(np.float32)
    vmem = pl.BlockSpec(memory_space=pltpu.VMEM)
    half_ring = n_roll // 4
    bf16, f32 = jnp.bfloat16, jnp.float32
    dma = pltpu.SemaphoreType.DMA
    out = pl.pallas_call(
        functools.partial(kernel, n_roll, n_seq),
        out_shape=jax.ShapeDtypeStruct((q_rows, q_width), bf16),
        in_specs=[
            pl.BlockSpec(memory_space=pltpu.SMEM),
            vmem,
            pl.BlockSpec(memory_space=pl.ANY),
            vmem,
            vmem,
            vmem,
            vmem,
            vmem,
        ],
        out_specs=vmem,
        scratch_shapes=[
            pltpu.VMEM((n_roll, depth, columns), bf16),
            pltpu.VMEM((rows, model_width), bf16),
            pltpu.VMEM((n_roll, rows, depth), bf16),
            pltpu.VMEM((rows, columns), f32),
            pltpu.VMEM((half, rows), f32),
            pltpu.VMEM((half, rows), f32),
            pltpu.VMEM((heads, 128, rows), bf16),
            pltpu.VMEM((heads, rows, 256), bf16),
            pltpu.VMEM((n_seq, q_rows, q_width), bf16),
            pltpu.VMEM((n_seq, q_rows, 128), f32),
            pltpu.VMEM((n_seq, q_rows, q_width), bf16),
            pltpu.VMEM((n_seq, q_rows, q_width), bf16),
            pltpu.VMEM((n_seq, q_rows, 128), f32),
            pltpu.VMEM((n_seq, q_rows, 128), f32),
            pltpu.VMEM((q_rows, q_width), f32),
            pltpu.VMEM((q_rows, 128), f32),
            dma,
            dma((2, 2, half_ring)),
            dma((2, 2, half_ring)),
            dma((2, 2, half_ring + 1)),
            dma((2, 2, half_ring + 1)),
            dma((n_seq,)),
            dma((n_seq,)),
            dma((n_seq,)),
            dma((n_seq,)),
            dma((n_seq, heads)),
            dma((n_seq, heads)),
            dma((n_seq,)),
            dma((n_seq,)),
        ],
        compiler_params=pltpu.CompilerParams(
            collective_id=0, has_side_effects=True, vmem_limit_bytes=52 * 1024 * 1024
        ),
        cost_estimate=pl.CostEstimate(
            flops=2 * rows * model_width * columns,
            bytes_accessed=2 * rows * model_width,
            transcendentals=0,
        ),
    )(
        block_of,
        key_value_blocks,
        hidden[0],
        queries[0],
        key_pos,
        query_pos,
        jnp.asarray(freq[:, None]),
        jnp.asarray(np.tile(freq, 128 // half)[None]),
    )
    return out[None]


def solution(mesh):
    return jax.shard_map(
        functools.partial(shards, mesh.shape["roll"], mesh.shape["seq"]),
        mesh=mesh,
        in_specs=(
            P("roll", "seq", None),
            P("roll", None),
            P(),
            P("roll", "seq", None),
            P("roll", "seq"),
            P("roll", "seq"),
        ),
        out_specs=P("roll", "seq", None),
        check_vma=False,
    )
```

time: 200 us -> 61.5 us (0.31)
  Pallas kernels: 0 us -> 55.8 us
  waiting for transfers between devices: 53 us -> 0 us
  matrix products: 37.5 us -> 0 us
  local copies, waits for them, and re-layouts: 36.7 us -> 5.41 us
  blocking collectives: 24.9 us -> 0 us
  loops' own time: 18.5 us -> 0 us
  between operations: 14.2 us -> 0.07 us
  starting transfers between devices: 7.82 us -> 0 us
  other arithmetic: 6.19 us -> 0 us
    pallas_call x0 -> x1, Pallas kernels: none -> 55.8 us  [shards(): pl.pallas_call(functools.partial(kernel, n_roll, n_seq), out_shape=jax.Sh...]
    all_gather x1 -> x0, waiting for transfers between devices: 52.3 us -> none  [shards(): piece = lax.all_gather(key_value_blocks, 'roll', axis=0, tiled=True)]
    dot_general x24 -> x0, matrix products: 37.5 us -> none  [the longest x16 31.3 us: one_block(): jnp.dot(hidden_cols, weight_rows, preferred_element_type=jnp.float32)]
    another operation x2 -> x0, loops' own time: 18.5 us -> none  [the longest x1 10.7 us: shards(): lax.fori_loop(0, count, one_block, jnp.zeros((row_count, all_columns), jn...]
    all_gather x2 -> x0, blocking collectives: 17.3 us -> none  [the longest x1 13 us: shards(): lax.all_gather(query_pos[0], 'seq', axis=0, tiled=True)]
    dynamic_slice x24 -> x0, local copies, waits for them, and re-layouts: 12.8 us -> none  [the longest x16 10.2 us: one_block(): logical = block_of[offset]]
    unnamed x13 -> x16, local copies, waits for them, and re-layouts: 13.3 us -> 5.41 us
    all_to_all x2 -> x0, starting transfers between devices: 7.81 us -> none  [the longest x1 4.23 us: shards(): lax.all_to_all(rotated_rows, 'seq', split_axis=1, concat_axis=0, tiled=True)]
  transfers between devices with their start and end apart: 3 -> 0, of which waited for: 1 -> 0; matrix products, arithmetic and copies ran while one was open for 33% -> 0% of each run, Pallas kernels for 0% -> 0%
where the time goes in v1:
time: 61.5 us; the launch traced here: 61.3 us
  Pallas kernels  55.8 us (91%)
  local copies, waits for them, and re-layouts  5.41 us (9%)
    pallas_call x1, Pallas kernels, shards(): pl.pallas_call(functools.partial(kernel, n_roll, n_seq), out_shape=jax.Sh...  55.8 us
    unnamed x16, local copies, waits for them, and re-layouts  5.41 us

profile of v1, /device:TPU:0, one launch (start us, length us, event | category | flops | bytes accessed | tf_op | source)
XLA Modules:
  0.0 61.3 jit_solution(4675393645903537604)
XLA Ops:
  0.0 0.0 copy-start.6
  0.0 0.0 copy-start.5
  0.0 0.0 copy-start.4
  0.0 0.0 copy-start.2
  0.0 0.0 copy-start.1
  0.0 0.0 copy-start.3
  0.0 0.0 copy-start
  0.0 4.7 %copy.9 = bf16[1,512,2880]{2,1,0:T(8,128)(2,1)} copy(bf16[1,512,2880]{1,2,0:T(8,128)(2,1)} %param.8) | data formatting | bytes 5898240 | tf_op args[0]
  4.7 0.0 copy-done.6
  4.7 0.0 copy-done.5
  4.7 0.0 copy-done.4
  4.7 0.0 copy-done.2
  4.7 0.0 copy-done.1
  4.7 0.0 copy-done.3
  4.7 0.0 copy-done
  4.8 55.8 %shard_map.82 = bf16[32,4096]{1,0:T(8,128)(2,1)S(1)} custom-call(s32[16]{0:T(128)S(1)} %copy-done.3, bf16[180,1024]{1,0:T(8,128)(2,1)S(1)} %copy-done, bf16[512,2880]{1,0:T(8,128)(2,1)} %bitcast.5, bf16[32,4096]{1,0:T(8,128)(2,1)S(1)} %bitcast.4, s32[1,512]{1,0:T(1,128)S(1)} %copy-done.2, s32[1,32]{1,0:T(1,128)S(1)} %copy-done.4, f32[32,1]{1,0:T(8,128)S(1)} %copy-done.5, ...), custom_call_target="tpu_custom_call" | custom-call | flops 3019898880 | bytes 2949120 | tf_op jit(solution)/shard_map/pallas_call | solution.py:433
  60.5 0.7 %copy.11 = bf16[1,32,4096]{2,1,0:T(8,128)(2,1)} copy(bf16[1,32,4096]{2,1,0:T(8,128)(2,1)S(1)} %bitcast.3) | data formatting | bytes 524288
Async XLA Ops:
  0.0 4.7 %copy-start.6 = (f32[1,128]{1,0:T(1,128)S(1)}, f32[1,128]{1,0:T(1,128)}, u32[]{:S(2)}) copy-start(f32[1,128]{1,0:T(1,128)} %constant.5.clone.freq_row_ref) | copy-start | bytes 1540
  0.0 4.7 %copy-start.5 = (f32[32,1]{1,0:T(8,128)S(1)}, f32[32,1]{1,0:T(8,128)}, u32[]{:S(2)}) copy-start(f32[32,1]{1,0:T(8,128)} %constant.4.clone.freq_col_ref) | copy-start | bytes 388
  0.0 4.7 %copy-start.4 = (s32[1,32]{1,0:T(1,128)S(1)}, s32[1,32]{1,0:T(1,128)}, u32[]{:S(2)}) copy-start(s32[1,32]{1,0:T(1,128)} %query_pos_ref.1) | copy-start | bytes 388
  0.0 4.7 %copy-start.2 = (s32[1,512]{1,0:T(1,128)S(1)}, s32[1,512]{1,0:T(1,128)}, u32[]{:S(2)}) copy-start(s32[1,512]{1,0:T(1,128)} %key_pos_ref.1) | copy-start | bytes 6148
  0.0 4.7 %copy-start.1 = (bf16[1,32,4096]{2,1,0:T(8,128)(2,1)S(1)}, bf16[1,32,4096]{2,1,0:T(8,128)(2,1)}, u32[]{:S(2)}) copy-start(bf16[1,32,4096]{2,1,0:T(8,128)(2,1)} %param.11) | copy-start | bytes 786436
  0.0 4.7 %copy-start.3 = (s32[16]{0:T(128)S(1)}, s32[16]{0:T(128)}, u32[]{:S(2)}) copy-start(s32[16]{0:T(128)} %block_of.1) | copy-start | bytes 196
  0.0 4.7 %copy-start = (bf16[180,1024]{1,0:T(8,128)(2,1)S(1)}, bf16[180,1024]{1,0:T(8,128)(2,1)}, u32[]{:S(2)}) copy-start(bf16[180,1024]{1,0:T(8,128)(2,1)} %w_ref.1) | copy-start | bytes 1105924

commit v2 on v1

--- a/solution.py
+++ b/solution.py
@@ -32,8 +32,6 @@
     acc,
     cos_k,
     sin_k,
-    kk,
-    vv,
     q_all,
     qpos_all,
     o_send,
@@ -41,12 +39,13 @@
     l_send,
     l_recv,
     o_own,
-    l_own,
     hidden_sem,
     ring_send,
     ring_recv,
     sib_send,
     sib_recv,
+    own_send,
+    own_recv,
     q_send_sem,
     q_recv_sem,
     qp_send_sem,
@@ -57,16 +56,16 @@
     l_recv_sem,
 ):
     depth, columns = w_ref.shape
-    rows = hidden_vm.shape[0]
+    rows = hidden_vm.shape[1]
     q_rows, q_width = q_ref.shape
     heads = columns // (2 * HEAD_WIDTH)
     group = q_width // HEAD_WIDTH // heads
     group_width = group * HEAD_WIDTH
     ring = n_roll // 2
     half_ring = ring // 2
-    phases = 2
+    phase_heads = 2
+    phases = heads // phase_heads
     width = columns // phases
-    heads_per_phase = heads // phases
 
     me = lax.axis_index("roll")
     seq = lax.axis_index("seq")
@@ -98,17 +97,23 @@
     hidden_copy = pltpu.make_async_copy(hidden_ref, hidden_vm, hidden_sem)
     hidden_copy.start()
 
-    def cols(phase, part):
+    def cols(phase):
+        return pl.ds(phase * width, width)
+
+    def some_heads(phase, part):
         if part is None:
-            return pl.ds(phase * width, width)
-        return pl.ds(phase * width + part * (width // 2), width // 2)
-
-    def ring_copy(phase, direction, step, part, own=False):
-        origin = roll_of(place - (step - 1) * (1 - 2 * direction), core)
-        c = cols(phase, part)
+            return pl.ds(phase * phase_heads, phase_heads)
+        return pl.ds(phase * phase_heads + part, 1)
+
+    def origin_of(direction, step, which_core):
+        return roll_of(place - step * (1 - 2 * direction), which_core)
+
+    def ring_copy(phase, direction, step, part, arrival=False):
+        origin = origin_of(direction, step if arrival else step - 1, core)
+        block = w_all.at[origin, some_heads(phase, part)]
         return pltpu.make_async_remote_copy(
-            src_ref=w_ref.at[:, c] if own else w_all.at[origin, :, c],
-            dst_ref=w_all.at[origin, :, c],
+            src_ref=block,
+            dst_ref=block,
             send_sem=ring_send.at[phase, direction, step - 1],
             recv_sem=ring_recv.at[phase, direction, step - 1],
             device_id=(right if direction == 0 else left, seq),
@@ -116,35 +121,39 @@
         )
 
     def ring_arrival(phase, direction, step, part):
-        origin = roll_of(place - step * (1 - 2 * direction), core)
-        c = cols(phase, part)
+        return ring_copy(phase, direction, step, part, arrival=True)
+
+    def sib_copy(phase, direction, step, part, which_core):
+        block = w_all.at[origin_of(direction, step, which_core), some_heads(phase, part)]
         return pltpu.make_async_remote_copy(
-            src_ref=w_all.at[origin, :, c],
-            dst_ref=w_all.at[origin, :, c],
-            send_sem=ring_send.at[phase, direction, step - 1],
-            recv_sem=ring_recv.at[phase, direction, step - 1],
-            device_id=(right if direction == 0 else left, seq),
-            device_id_type=MESH,
-        )
-
-    def sib_copy(phase, direction, step, part, which_core, own=False):
-        origin = roll_of(place - step * (1 - 2 * direction), which_core)
-        c = cols(phase, part)
-        return pltpu.make_async_remote_copy(
-            src_ref=w_ref.at[:, c] if own else w_all.at[origin, :, c],
-            dst_ref=w_all.at[origin, :, c],
-            send_sem=sib_send.at[phase, direction, step],
-            recv_sem=sib_recv.at[phase, direction, step],
+            src_ref=block,
+            dst_ref=block,
+            send_sem=sib_send.at[phase, direction, step - 1],
+            recv_sem=sib_recv.at[phase, direction, step - 1],
             device_id=(sibling, seq),
             device_id_type=MESH,
         )
 
+    def sib_own(origin):
+        return pltpu.make_async_remote_copy(
+            src_ref=w_all.at[origin],
+            dst_ref=w_all.at[origin],
+            send_sem=own_send,
+            recv_sem=own_recv,
+            device_id=(sibling, seq),
+            device_id_type=MESH,
+        )
+
+    for h in range(heads):
+        w_all[me, h] = w_ref[:, h * 128 : (h + 1) * 128]
+
     def start_phase(phase):
         for direction in range(2):
-            ring_copy(phase, direction, 1, None if half_ring > 1 else direction, own=True).start()
-        sib_copy(phase, 0, 0, None, core, own=True).start()
+            ring_copy(phase, direction, 1, None).start()
 
     start_phase(0)
+    sib_own(me).start()
+    start_phase(1)
 
     lane = lax.broadcasted_iota(jnp.int32, (q_rows, 128), 1)
     on_diag = lax.broadcasted_iota(jnp.int32, (q_rows, q_rows), 0) == lax.broadcasted_iota(
@@ -207,88 +216,16 @@
 
     hidden_copy.wait()
     for b in range(n_roll):
-        h_blocks[b] = hidden_vm[:, b * depth : (b + 1) * depth]
-
-    def multiply(block, phase, own=False, first=False):
-        logical = block_of[block]
-        c = cols(phase, None)
-        weights = w_ref[:, c] if own else w_all[block, :, c]
-        product = jnp.dot(h_blocks[logical], weights, preferred_element_type=jnp.float32)
-        if first:
-            acc[:, c] = product
-        else:
-            acc[:, c] += product
-
-    for phase in range(phases):
-        multiply(me, phase, own=True, first=True)
-
-        def step_body(step, carry):
-            for direction in range(2):
-                ring_arrival(phase, direction, step, None).wait_recv()
-
-                if half_ring > 2:
-
-                    @pl.when(step < half_ring - 1)
-                    def _():
-                        ring_copy(phase, direction, step + 1, None).start()
-
-                @pl.when(step == half_ring - 1)
-                def _():
-                    ring_copy(phase, direction, step + 1, direction).start()
-
-                sib_copy(phase, direction, step, None, core).start()
-            multiply(roll_of(place - step, core), phase)
-            multiply(roll_of(place + step, core), phase)
-
-            @pl.when(step == 1)
-            def _():
-                sib_copy(phase, 0, 0, None, 1 - core).wait_recv()
-                multiply(sibling, phase)
-
-            @pl.when(step > 1)
-            def _():
-                for direction in range(2):
-                    sib_copy(phase, direction, step - 1, None, 1 - core).wait_recv()
-                    multiply(
-                        roll_of(place - (step - 1) * (1 - 2 * direction), 1 - core), phase
-                    )
-
-            return carry
-
-        lax.fori_loop(1, half_ring, step_body, 0)
-        if phase + 1 < phases:
-            start_phase(phase + 1)
-        for direction in range(2):
-            ring_arrival(phase, direction, half_ring, direction).wait_recv()
-            sib_copy(phase, direction, half_ring, direction, core).start()
-        for direction in range(2):
-            sib_copy(phase, direction, half_ring - 1, None, 1 - core).wait_recv()
-            multiply(
-                roll_of(place - (half_ring - 1) * (1 - 2 * direction), 1 - core), phase
-            )
-        multiply(roll_of(place + half_ring, core), phase)
-        for direction in range(2):
-            sib_copy(phase, direction, half_ring, direction, 1 - core).wait_recv()
-        multiply(roll_of(place + half_ring, 1 - core), phase)
-
-    lane_k = lax.broadcasted_iota(jnp.int32, (rows, 128), 1)
-    cos_keys = cos_k[...]
-    sin_keys = sin_k[...]
-
-    def prepare(h, carry):
-        both = acc[:, pl.ds(pl.multiple_of(h * 128, 128), 128)]
-        turned = both.T
-        first = turned[: HEAD_WIDTH // 2]
-        second = turned[HEAD_WIDTH // 2 : HEAD_WIDTH]
-        key = jnp.concatenate(
-            [first * cos_keys - second * sin_keys, second * cos_keys + first * sin_keys], axis=0
-        )
-        kk[h] = jnp.concatenate([key, key], axis=0).astype(jnp.bfloat16)
-        value = jnp.where(lane_k < HEAD_WIDTH, pltpu.roll(both, HEAD_WIDTH, 1), both)
-        vv[h] = jnp.concatenate([value, jnp.ones_like(value)], axis=1).astype(jnp.bfloat16)
-        return carry
-
-    lax.fori_loop(0, heads, prepare, 0)
+        h_blocks[b] = hidden_vm[b * depth : (b + 1) * depth, :].T
+
+    def product(block, phase):
+        weights = jnp.concatenate(
+            [w_all[block, phase * phase_heads + j] for j in range(phase_heads)], axis=1
+        )
+        return jnp.dot(h_blocks[block_of[block]], weights, preferred_element_type=jnp.float32)
+
+    def multiply(block, phase):
+        acc[:, cols(phase)] += product(block, phase)
 
     def o_copy(i, h):
         c = pl.ds(pl.multiple_of(h * group_width, group_width), group_width)
@@ -314,25 +251,27 @@
     left_lanes = lane < HEAD_WIDTH
     pairs = group // 2
 
-    def attend(i, h, allowed, packed):
+    def attend(i, h, keys, values):
         target = (seq + i) % n_seq
-        base = pl.multiple_of(h * group_width, group_width)
-        queries = q_all[target, :, pl.ds(base, group_width)]
+        base = h * group_width
+        queries = q_all[target, :, pl.ds(pl.multiple_of(base, group_width), group_width)]
         parts = []
         for j in range(pairs):
             two = queries[:, j * 128 : (j + 1) * 128]
             parts.append(jnp.where(left_lanes, two, jnp.zeros_like(two)))
             parts.append(jnp.where(left_lanes, jnp.zeros_like(two), two))
         stacked = jnp.concatenate(parts, axis=0)
-        scores = jnp.dot(stacked, kk[h], preferred_element_type=jnp.float32)
+        allowed = k_pos <= qpos_all[target][:, 0:1]
+        scores = jnp.dot(stacked, keys, preferred_element_type=jnp.float32)
         scores = scores.reshape(group, q_rows, rows)
         scores = jnp.where(allowed[None], scores, MASKED).reshape(group * q_rows, rows)
         top = jnp.max(scores, axis=1, keepdims=True)
         probs = jnp.exp(scores - top).astype(jnp.bfloat16)
-        result = jnp.dot(probs, vv[h], preferred_element_type=jnp.float32)
+        result = jnp.dot(probs, values, preferred_element_type=jnp.float32)
         total = result[:, 128:]
         normal = result[:, :128] / total
         logs = top + jnp.log(total)
+        packed = l_send[i]
         for j in range(pairs):
             even = slice(2 * j * q_rows, (2 * j + 1) * q_rows)
             odd = slice((2 * j + 1) * q_rows, (2 * j + 2) * q_rows)
@@ -344,29 +283,90 @@
                 o_send[i, :, c] = tile.astype(jnp.bfloat16)
             packed = jnp.where(lane == h * group + 2 * j, logs[even], packed)
             packed = jnp.where(lane == h * group + 2 * j + 1, logs[odd], packed)
-        return packed
-
-    for i in list(range(1, n_seq)) + [0]:
-        if i:
-            for copy in q_copies(i, (seq - i + n_seq) % n_seq):
-                copy.wait_recv()
-
-    for i in list(range(1, n_seq)) + [0]:
-        target = (seq + i) % n_seq
-        allowed = k_pos <= qpos_all[target][:, 0:1]
-
-        def one_head(h, packed):
-            packed = attend(i, h, allowed, packed)
-            if i:
-                o_copy(i, h).start()
-            return packed
-
-        packed = lax.fori_loop(0, heads, one_head, jnp.zeros((q_rows, 128), jnp.float32))
-        if i:
-            l_send[i] = packed
-            l_copy(i).start()
-        else:
-            l_own[...] = packed
+        l_send[i] = packed
+
+    l_send[...] = jnp.zeros_like(l_send)
+    lane_k = lax.broadcasted_iota(jnp.int32, (rows, 128), 1)
+
+    def one_head(h):
+        both = acc[:, pl.ds(pl.multiple_of(h * 128, 128), 128)]
+        turned = both.T
+        first = turned[: HEAD_WIDTH // 2]
+        second = turned[HEAD_WIDTH // 2 : HEAD_WIDTH]
+        cos_keys = cos_k[...]
+        sin_keys = sin_k[...]
+        key = jnp.concatenate(
+            [first * cos_keys - second * sin_keys, second * cos_keys + first * sin_keys], axis=0
+        )
+        keys = jnp.concatenate([key, key], axis=0).astype(jnp.bfloat16)
+        value = jnp.where(lane_k < HEAD_WIDTH, pltpu.roll(both, HEAD_WIDTH, 1), both)
+        values = jnp.concatenate([value, jnp.ones_like(value)], axis=1).astype(jnp.bfloat16)
+        for i in list(range(1, n_seq)) + [0]:
+            attend(i, h, keys, values)
+        for i in range(1, n_seq):
+            o_copy(i, h).start()
+
+    in_loop = min(phase_heads, half_ring - 1)
+    for phase in range(phases):
+        acc[:, cols(phase)] = product(me, phase)
+
+        def step_body(step, carry):
+            for direction in range(2):
+                ring_arrival(phase, direction, step, None).wait_recv()
+
+                @pl.when(step < half_ring - 1)
+                def _():
+                    ring_copy(phase, direction, step + 1, None).start()
+
+                @pl.when(step == half_ring - 1)
+                def _():
+                    ring_copy(phase, direction, step + 1, direction).start()
+
+                sib_copy(phase, direction, step, None, core).start()
+            multiply(origin_of(0, step, core), phase)
+            multiply(origin_of(1, step, core), phase)
+
+            @pl.when(step > 1)
+            def _():
+                for direction in range(2):
+                    sib_copy(phase, direction, step - 1, None, 1 - core).wait_recv()
+                    multiply(origin_of(direction, step - 1, 1 - core), phase)
+
+            if phase > 0:
+
+                @pl.when(step <= in_loop)
+                def _():
+                    one_head((phase - 1) * phase_heads + step - 1)
+
+            return carry
+
+        lax.fori_loop(1, half_ring, step_body, 0)
+        if phase + 2 < phases:
+            start_phase(phase + 2)
+        if phase == 0:
+            sib_own(sibling).wait_recv()
+            for i in range(1, n_seq):
+                for copy in q_copies(i, (seq - i + n_seq) % n_seq):
+                    copy.wait_recv()
+        multiply(sibling, phase)
+        for direction in range(2):
+            sib_copy(phase, direction, half_ring - 1, None, 1 - core).wait_recv()
+            multiply(origin_of(direction, half_ring - 1, 1 - core), phase)
+        for direction in range(2):
+            ring_arrival(phase, direction, half_ring, direction).wait_recv()
+            sib_copy(phase, direction, half_ring, direction, core).start()
+        multiply(origin_of(0, half_ring, core), phase)
+        if phase > 0:
+            for left_over in range(in_loop, phase_heads):
+                one_head((phase - 1) * phase_heads + left_over)
+        for direction in range(2):
+            sib_copy(phase, direction, half_ring, direction, 1 - core).wait_recv()
+        multiply(origin_of(0, half_ring, 1 - core), phase)
+
+    for j in range(phase_heads):
+        one_head((phases - 1) * phase_heads + j)
+    for i in range(1, n_seq):
+        l_copy(i).start()
 
     for i in range(1, n_seq):
         l_copy(i).wait_recv()
@@ -377,7 +377,7 @@
 
         lax.fori_loop(0, heads, wait_head, 0)
 
-    logs = [l_own[...]] + [l_recv[i] for i in range(1, n_seq)]
+    logs = [l_send[0]] + [l_recv[i] for i in range(1, n_seq)]
     top = functools.reduce(jnp.maximum, logs)
     shares = [jnp.exp(entry - top) for entry in logs]
     whole = functools.reduce(jnp.add, shares)
@@ -403,8 +403,8 @@
             return carry
 
         lax.fori_loop(0, heads, sent_head, 0)
+    sib_own(me).wait_send()
     for phase in range(phases):
-        sib_copy(phase, 0, 0, None, core, own=True).wait_send()
 
         def sent_step(step, carry):
             for direction in range(2):
@@ -428,6 +428,7 @@
     freq = freq.astype(np.float32)
     vmem = pl.BlockSpec(memory_space=pltpu.VMEM)
     half_ring = n_roll // 4
+    phases = heads // 2
     bf16, f32 = jnp.bfloat16, jnp.float32
     dma = pltpu.SemaphoreType.DMA
     out = pl.pallas_call(
@@ -445,14 +446,12 @@
         ],
         out_specs=vmem,
         scratch_shapes=[
-            pltpu.VMEM((n_roll, depth, columns), bf16),
-            pltpu.VMEM((rows, model_width), bf16),
+            pltpu.VMEM((n_roll, heads, depth, 128), bf16),
+            pltpu.VMEM((model_width, rows), bf16),
             pltpu.VMEM((n_roll, rows, depth), bf16),
             pltpu.VMEM((rows, columns), f32),
             pltpu.VMEM((half, rows), f32),
             pltpu.VMEM((half, rows), f32),
-            pltpu.VMEM((heads, 128, rows), bf16),
-            pltpu.VMEM((heads, rows, 256), bf16),
             pltpu.VMEM((n_seq, q_rows, q_width), bf16),
             pltpu.VMEM((n_seq, q_rows, 128), f32),
             pltpu.VMEM((n_seq, q_rows, q_width), bf16),
@@ -460,12 +459,13 @@
             pltpu.VMEM((n_seq, q_rows, 128), f32),
             pltpu.VMEM((n_seq, q_rows, 128), f32),
             pltpu.VMEM((q_rows, q_width), f32),
-            pltpu.VMEM((q_rows, 128), f32),
             dma,
-            dma((2, 2, half_ring)),
-            dma((2, 2, half_ring)),
-            dma((2, 2, half_ring + 1)),
-            dma((2, 2, half_ring + 1)),
+            dma((phases, 2, half_ring)),
+            dma((phases, 2, half_ring)),
+            dma((phases, 2, half_ring)),
+            dma((phases, 2, half_ring)),
+            dma,
+            dma,
             dma((n_seq,)),
             dma((n_seq,)),
             dma((n_seq,)),
@@ -486,7 +486,7 @@
     )(
         block_of,
         key_value_blocks,
-        hidden[0],
+        hidden[0].T,
         queries[0],
         key_pos,
         query_pos,

time: 61.5 us -> 71.4 us (1.16)
  Pallas kernels: 55.8 us -> 65.1 us
    pallas_call x1, Pallas kernels: 55.8 us -> 65.1 us  [shards(): pl.pallas_call(functools.partial(kernel, n_roll, n_seq), out_shape=jax.Sh...]
    unnamed x16 -> x15, local copies, waits for them, and re-layouts: 5.41 us -> 6.01 us
where the time goes in v2:
time: 71.4 us; the launch traced here: 71.1 us
  Pallas kernels  65.1 us (91%)
  local copies, waits for them, and re-layouts  6.01 us (8%)
    pallas_call x1, Pallas kernels, shards(): pl.pallas_call(functools.partial(kernel, n_roll, n_seq), out_shape=jax.Sh...  65.1 us
    unnamed x15, local copies, waits for them, and re-layouts  6.01 us

profile of v2, /device:TPU:0, one launch (start us, length us, event | category | flops | bytes accessed | tf_op | source)
XLA Modules:
  0.0 71.1 jit_solution(9708817540067055073)
XLA Ops:
  0.0 0.0 copy-start
  0.0 1.0 %copy-done = bf16[180,1024]{1,0:T(8,128)(2,1)S(1)} copy-done((bf16[180,1024]{1,0:T(8,128)(2,1)S(1)}, bf16[180,1024]{1,0:T(8,128)(2,1)}, u32[]{:S(2)}) %copy-start) | copy-done | bytes 368664
  1.0 0.0 copy-start.1
  1.0 0.9 %copy-done.1 = bf16[1,32,4096]{2,1,0:T(8,128)(2,1)S(1)} copy-done((bf16[1,32,4096]{2,1,0:T(8,128)(2,1)S(1)}, bf16[1,32,4096]{2,1,0:T(8,128)(2,1)}, u32[]{:S(2)}) %copy-start.1) | copy-done | bytes 262168
  1.9 0.0 copy-start.2
  1.9 0.7 copy-done.2
  2.6 0.0 copy-start.3
  2.6 0.7 copy-done.3
  3.3 0.0 copy-start.4
  3.3 0.7 copy-done.4
  3.9 0.0 copy-start.5
  3.9 0.7 %copy-done.5 = f32[32,1]{1,0:T(8,128)S(1)} copy-done((f32[32,1]{1,0:T(8,128)S(1)}, f32[32,1]{1,0:T(8,128)}, u32[]{:S(2)}) %copy-start.5) | copy-done | bytes 152
  4.7 0.0 copy-start.6
  4.7 0.7 copy-done.6
  5.3 65.1 %shard_map.82 = bf16[32,4096]{1,0:T(8,128)(2,1)S(1)} custom-call(s32[16]{0:T(128)S(1)} %copy-done.3, bf16[180,1024]{1,0:T(8,128)(2,1)S(1)} %copy-done, bf16[2880,512]{1,0:T(8,128)(2,1)} %bitcast.7, bf16[32,4096]{1,0:T(8,128)(2,1)S(1)} %bitcast.6, s32[1,512]{1,0:T(1,128)S(1)} %copy-done.2, s32[1,32]{1,0:T(1,128)S(1)} %copy-done.4, f32[32,1]{1,0:T(8,128)S(1)} %copy-done.5, ...), custom_call_target="tpu_custom_call" | custom-call | flops 3019898880 | bytes 2949120 | tf_op jit(solution)/shard_map/pallas_call | solution.py:434
  70.4 0.7 copy.10
Async XLA Ops:
  0.0 1.0 %copy-start = (bf16[180,1024]{1,0:T(8,128)(2,1)S(1)}, bf16[180,1024]{1,0:T(8,128)(2,1)}, u32[]{:S(2)}) copy-start(bf16[180,1024]{1,0:T(8,128)(2,1)} %w_ref.1) | copy-start | bytes 1105924
  1.0 0.9 %copy-start.1 = (bf16[1,32,4096]{2,1,0:T(8,128)(2,1)S(1)}, bf16[1,32,4096]{2,1,0:T(8,128)(2,1)}, u32[]{:S(2)}) copy-start(bf16[1,32,4096]{2,1,0:T(8,128)(2,1)} %param.11) | copy-start | bytes 786436
  1.9 0.7 copy-start.2
  2.6 0.7 copy-start.3
  3.3 0.7 copy-start.4
  3.9 0.7 %copy-start.5 = (f32[32,1]{1,0:T(8,128)S(1)}, f32[32,1]{1,0:T(8,128)}, u32[]{:S(2)}) copy-start(f32[32,1]{1,0:T(8,128)} %constant.4.clone.freq_col_ref) | copy-start | bytes 388
  4.7 0.7 copy-start.6

commit v3 on v2

--- a/solution.py
+++ b/solution.py
@@ -1,4 +1,5 @@
 import functools
+import math
 
 import jax
 import jax.numpy as jnp
@@ -14,21 +15,30 @@
 rope_base = 150000.0
 
 
+def phase_plan(heads):
+    return ((0, heads // 2), (heads // 2, heads // 4), (heads // 2 + heads // 4, heads // 4))
+
+
 def kernel(
     n_roll,
     n_seq,
     block_of,
     w_ref,
     hidden_ref,
+    q_hbm,
+    key_pos_hbm,
+    query_pos_hbm,
+    freq_hbm,
+    out_ref,
     q_ref,
     key_pos_ref,
     query_pos_ref,
-    freq_col_ref,
-    freq_row_ref,
-    out_ref,
+    freq_ref,
     w_all,
     hidden_vm,
     h_blocks,
+    h_all,
+    w_phase,
     acc,
     cos_k,
     sin_k,
@@ -40,6 +50,8 @@
     l_recv,
     o_own,
     hidden_sem,
+    small_sem,
+    w_sem,
     ring_send,
     ring_recv,
     sib_send,
@@ -58,14 +70,13 @@
     depth, columns = w_ref.shape
     rows = hidden_vm.shape[1]
     q_rows, q_width = q_ref.shape
+    padded = h_blocks.shape[1]
     heads = columns // (2 * HEAD_WIDTH)
     group = q_width // HEAD_WIDTH // heads
     group_width = group * HEAD_WIDTH
     ring = n_roll // 2
     half_ring = ring // 2
-    phase_heads = 2
-    phases = heads // phase_heads
-    width = columns // phases
+    phases = phase_plan(heads)
 
     me = lax.axis_index("roll")
     seq = lax.axis_index("seq")
@@ -85,6 +96,25 @@
     left = roll_of(place - 1, core)
     sibling = 2 * chip + 1 - core
 
+    w_copies = [
+        pltpu.make_async_copy(w_ref.at[:, pl.ds(h * 128, 128)], w_all.at[me, h], w_sem.at[h])
+        for h in range(heads)
+    ]
+    small_copies = [
+        pltpu.make_async_copy(source, target, small_sem.at[n])
+        for n, (source, target) in enumerate(
+            (
+                (q_hbm, q_ref),
+                (query_pos_hbm, query_pos_ref),
+                (freq_hbm, freq_ref),
+                (key_pos_hbm, key_pos_ref),
+            )
+        )
+    ]
+    hidden_copy = pltpu.make_async_copy(hidden_ref, hidden_vm, hidden_sem)
+    for copy in w_copies + small_copies + [hidden_copy]:
+        copy.start()
+
     barrier = pltpu.get_barrier_semaphore()
     for other in (left, right, sibling):
         pl.semaphore_signal(barrier, inc=1, device_id=(other, seq), device_id_type=MESH)
@@ -94,16 +124,11 @@
         )
     pl.semaphore_wait(barrier, 3 + n_seq - 1)
 
-    hidden_copy = pltpu.make_async_copy(hidden_ref, hidden_vm, hidden_sem)
-    hidden_copy.start()
-
-    def cols(phase):
-        return pl.ds(phase * width, width)
-
     def some_heads(phase, part):
+        first, count = phases[phase]
         if part is None:
-            return pl.ds(phase * phase_heads, phase_heads)
-        return pl.ds(phase * phase_heads + part, 1)
+            return pl.ds(first, count)
+        return pl.ds(first + part * (count // 2), count // 2)
 
     def origin_of(direction, step, which_core):
         return roll_of(place - step * (1 - 2 * direction), which_core)
@@ -144,16 +169,23 @@
             device_id_type=MESH,
         )
 
-    for h in range(heads):
-        w_all[me, h] = w_ref[:, h * 128 : (h + 1) * 128]
-
     def start_phase(phase):
         for direction in range(2):
             ring_copy(phase, direction, 1, None).start()
 
+    def wait_own(phase):
+        first, count = phases[phase]
+        for h in range(first, first + count):
+            w_copies[h].wait()
+
+    wait_own(0)
     start_phase(0)
+    for phase in range(1, len(phases)):
+        wait_own(phase)
     sib_own(me).start()
     start_phase(1)
+    for copy in small_copies:
+        copy.wait()
 
     lane = lax.broadcasted_iota(jnp.int32, (q_rows, 128), 1)
     on_diag = lax.broadcasted_iota(jnp.int32, (q_rows, q_rows), 0) == lax.broadcasted_iota(
@@ -166,7 +198,8 @@
         keepdims=True,
     )
     qpos_all[seq] = jnp.broadcast_to(q_pos_col, (q_rows, 128))
-    q_angle = q_pos_col * freq_row_ref[...]
+    freq_row = freq_ref[...]
+    q_angle = q_pos_col * freq_row
     q_cos = jnp.cos(q_angle)
     q_sin = jnp.sin(q_angle)
     first_half = lane % HEAD_WIDTH < HEAD_WIDTH // 2
@@ -210,22 +243,48 @@
             copy.start()
 
     k_pos = key_pos_ref[...].astype(jnp.float32)
-    k_angle = freq_col_ref[...] * k_pos
+    half = HEAD_WIDTH // 2
+    pick = lax.broadcasted_iota(jnp.int32, (half, 128), 0) == lax.broadcasted_iota(
+        jnp.int32, (half, 128), 1
+    )
+    freq_col = jnp.sum(
+        jnp.where(pick, jnp.broadcast_to(freq_row, (half, 128)), 0.0), axis=1, keepdims=True
+    )
+    k_angle = freq_col * k_pos
     cos_k[...] = jnp.cos(k_angle)
     sin_k[...] = jnp.sin(k_angle)
 
     hidden_copy.wait()
+    tail = padded - depth // 16 * 16
     for b in range(n_roll):
-        h_blocks[b] = hidden_vm[b * depth : (b + 1) * depth, :].T
-
-    def product(block, phase):
-        weights = jnp.concatenate(
-            [w_all[block, phase * phase_heads + j] for j in range(phase_heads)], axis=1
-        )
-        return jnp.dot(h_blocks[block_of[block]], weights, preferred_element_type=jnp.float32)
-
-    def multiply(block, phase):
-        acc[:, cols(phase)] += product(block, phase)
+        if padded > depth:
+            h_blocks[b, padded - tail :, :] = jnp.zeros((tail, rows), jnp.bfloat16)
+        h_blocks[b, :depth, :] = hidden_vm[b * depth : (b + 1) * depth, :]
+    together = 128 // math.gcd(padded, 128)
+    for b in range(0, n_roll, together):
+        turned = jnp.concatenate(
+            [h_blocks[block_of[b + n]] for n in range(together)], axis=0
+        ).T
+        h_all[:, b * padded : (b + together) * padded] = turned
+    if padded > depth:
+        for b in range(n_roll):
+            w_phase[(b + 1) * padded - tail : (b + 1) * padded, :] = jnp.zeros(
+                (tail, w_phase.shape[1]), jnp.bfloat16
+            )
+
+    def project(phase):
+        first, count = phases[phase]
+        for b in range(n_roll):
+            for j in range(count):
+                w_phase[b * padded : b * padded + depth, j * 128 : (j + 1) * 128] = w_all[
+                    b, first + j
+                ]
+        for j in range(0, count, 2):
+            acc[:, (first + j) * 128 : (first + j + 2) * 128] = jnp.dot(
+                h_all[...],
+                w_phase[:, j * 128 : (j + 2) * 128],
+                preferred_element_type=jnp.float32,
+            )
 
     def o_copy(i, h):
         c = pl.ds(pl.multiple_of(h * group_width, group_width), group_width)
@@ -306,9 +365,9 @@
         for i in range(1, n_seq):
             o_copy(i, h).start()
 
-    in_loop = min(phase_heads, half_ring - 1)
-    for phase in range(phases):
-        acc[:, cols(phase)] = product(me, phase)
+    for phase in range(len(phases)):
+        before, before_count = phases[phase - 1] if phase else (0, 0)
+        in_loop = min(before_count, half_ring - 1)
 
         def step_body(step, carry):
             for direction in range(2):
@@ -323,48 +382,42 @@
                     ring_copy(phase, direction, step + 1, direction).start()
 
                 sib_copy(phase, direction, step, None, core).start()
-            multiply(origin_of(0, step, core), phase)
-            multiply(origin_of(1, step, core), phase)
-
-            @pl.when(step > 1)
-            def _():
-                for direction in range(2):
-                    sib_copy(phase, direction, step - 1, None, 1 - core).wait_recv()
-                    multiply(origin_of(direction, step - 1, 1 - core), phase)
-
-            if phase > 0:
+
+            if in_loop:
 
                 @pl.when(step <= in_loop)
                 def _():
-                    one_head((phase - 1) * phase_heads + step - 1)
+                    one_head(before + step - 1)
 
             return carry
 
         lax.fori_loop(1, half_ring, step_body, 0)
-        if phase + 2 < phases:
+        if phase + 2 < len(phases):
             start_phase(phase + 2)
         if phase == 0:
             sib_own(sibling).wait_recv()
             for i in range(1, n_seq):
                 for copy in q_copies(i, (seq - i + n_seq) % n_seq):
                     copy.wait_recv()
-        multiply(sibling, phase)
-        for direction in range(2):
-            sib_copy(phase, direction, half_ring - 1, None, 1 - core).wait_recv()
-            multiply(origin_of(direction, half_ring - 1, 1 - core), phase)
         for direction in range(2):
             ring_arrival(phase, direction, half_ring, direction).wait_recv()
             sib_copy(phase, direction, half_ring, direction, core).start()
-        multiply(origin_of(0, half_ring, core), phase)
-        if phase > 0:
-            for left_over in range(in_loop, phase_heads):
-                one_head((phase - 1) * phase_heads + left_over)
+        for left_over in range(in_loop, before_count):
+            one_head(before + left_over)
+
+        def sib_step(step, carry):
+            for direction in range(2):
+                sib_copy(phase, direction, step, None, 1 - core).wait_recv()
+            return carry
+
+        lax.fori_loop(1, half_ring, sib_step, 0)
         for direction in range(2):
             sib_copy(phase, direction, half_ring, direction, 1 - core).wait_recv()
-        multiply(origin_of(0, half_ring, 1 - core), phase)
-
-    for j in range(phase_heads):
-        one_head((phases - 1) * phase_heads + j)
+        project(phase)
+
+    last, last_count = phases[-1]
+    for j in range(last_count):
+        one_head(last + j)
     for i in range(1, n_seq):
         l_copy(i).start()
 
@@ -404,7 +457,7 @@
 
         lax.fori_loop(0, heads, sent_head, 0)
     sib_own(me).wait_send()
-    for phase in range(phases):
+    for phase in range(len(phases)):
 
         def sent_step(step, carry):
             for direction in range(2):
@@ -428,7 +481,9 @@
     freq = freq.astype(np.float32)
     vmem = pl.BlockSpec(memory_space=pltpu.VMEM)
     half_ring = n_roll // 4
-    phases = heads // 2
+    phases = len(phase_plan(heads))
+    padded = -(-depth // 16) * 16
+    anywhere = pl.BlockSpec(memory_space=pl.ANY)
     bf16, f32 = jnp.bfloat16, jnp.float32
     dma = pltpu.SemaphoreType.DMA
     out = pl.pallas_call(
@@ -436,19 +491,24 @@
         out_shape=jax.ShapeDtypeStruct((q_rows, q_width), bf16),
         in_specs=[
             pl.BlockSpec(memory_space=pltpu.SMEM),
-            vmem,
-            pl.BlockSpec(memory_space=pl.ANY),
-            vmem,
-            vmem,
-            vmem,
-            vmem,
-            vmem,
+            anywhere,
+            anywhere,
+            anywhere,
+            anywhere,
+            anywhere,
+            anywhere,
         ],
         out_specs=vmem,
         scratch_shapes=[
+            pltpu.VMEM((q_rows, q_width), bf16),
+            pltpu.VMEM((1, rows), jnp.int32),
+            pltpu.VMEM((1, q_rows), jnp.int32),
+            pltpu.VMEM((1, 128), f32),
             pltpu.VMEM((n_roll, heads, depth, 128), bf16),
             pltpu.VMEM((model_width, rows), bf16),
-            pltpu.VMEM((n_roll, rows, depth), bf16),
+            pltpu.VMEM((n_roll, padded, rows), bf16),
+            pltpu.VMEM((rows, n_roll * padded), bf16),
+            pltpu.VMEM((n_roll * padded, columns // 2), bf16),
             pltpu.VMEM((rows, columns), f32),
             pltpu.VMEM((half, rows), f32),
             pltpu.VMEM((half, rows), f32),
@@ -460,6 +520,8 @@
             pltpu.VMEM((n_seq, q_rows, 128), f32),
             pltpu.VMEM((q_rows, q_width), f32),
             dma,
+            dma((4,)),
+            dma((heads,)),
             dma((phases, 2, half_ring)),
             dma((phases, 2, half_ring)),
             dma((phases, 2, half_ring)),
@@ -476,7 +538,7 @@
             dma((n_seq,)),
         ],
         compiler_params=pltpu.CompilerParams(
-            collective_id=0, has_side_effects=True, vmem_limit_bytes=52 * 1024 * 1024
+            collective_id=0, has_side_effects=True, vmem_limit_bytes=60 * 1024 * 1024
         ),
         cost_estimate=pl.CostEstimate(
             flops=2 * rows * model_width * columns,
@@ -490,7 +552,6 @@
         queries[0],
         key_pos,
         query_pos,
-        jnp.asarray(freq[:, None]),
         jnp.asarray(np.tile(freq, 128 // half)[None]),
     )
     return out[None]

time: 71.4 us -> 65.3 us (0.915)
  local copies, waits for them, and re-layouts: 6.01 us -> 1.67 us
  Pallas kernels: 65.1 us -> 63.4 us
    unnamed x15 -> x1, local copies, waits for them, and re-layouts: 6.01 us -> 1.67 us
    pallas_call x1, Pallas kernels: 65.1 us -> 63.4 us  [shards(): pl.pallas_call(functools.partial(kernel, n_roll, n_seq), out_shape=jax.Sh...]
where the time goes in v3:
time: 65.3 us; the launch traced here: 65.1 us
  Pallas kernels  63.4 us (97%)
  local copies, waits for them, and re-layouts  1.67 us (3%)
    pallas_call x1, Pallas kernels, shards(): pl.pallas_call(functools.partial(kernel, n_roll, n_seq), out_shape=jax.Sh...  63.4 us
    unnamed x1, local copies, waits for them, and re-layouts  1.67 us

profile of v3, /device:TPU:0, one launch (start us, length us, event | category | flops | bytes accessed | tf_op | source)
XLA Modules:
  0.0 65.1 jit_solution(17380548169900102774)
XLA Ops:
  0.0 63.4 %shard_map.73 = bf16[32,4096]{1,0:T(8,128)(2,1)} custom-call(s32[16]{0:T(128)} %block_of.1, bf16[180,1024]{1,0:T(8,128)(2,1)} %w_ref.1, bf16[2880,512]{1,0:T(8,128)(2,1)} %bitcast.6, bf16[32,4096]{1,0:T(8,128)(2,1)} %bitcast.7, s32[1,512]{1,0:T(1,128)} %key_pos_hbm.1, s32[1,32]{1,0:T(1,128)} %query_pos_hbm.1, f32[1,128]{1,0:T(1,128)} %constant.2.clone.freq_hbm), custom_call_target="tpu_custom_call" | custom-call | flops 3019898880 | bytes 2949120 | tf_op jit(solution)/shard_map/pallas_call | solution.py:489
  63.4 1.7 %copy.9 = bf16[1,32,4096]{2,1,0:T(8,128)(2,1)} copy(bf16[1,32,4096]{2,1,0:T(8,128)(2,1)} %bitcast.5) | data formatting | bytes 524288

commit v4 on v3

--- a/solution.py
+++ b/solution.py
@@ -16,7 +16,7 @@
 
 
 def phase_plan(heads):
-    return ((0, heads // 2), (heads // 2, heads // 4), (heads // 2 + heads // 4, heads // 4))
+    return tuple((first, 2) for first in range(0, heads, 2))
 
 
 def kernel(
@@ -251,28 +251,42 @@
         jnp.where(pick, jnp.broadcast_to(freq_row, (half, 128)), 0.0), axis=1, keepdims=True
     )
     k_angle = freq_col * k_pos
-    cos_k[...] = jnp.cos(k_angle)
-    sin_k[...] = jnp.sin(k_angle)
-
-    hidden_copy.wait()
     tail = padded - depth // 16 * 16
-    for b in range(n_roll):
-        if padded > depth:
-            h_blocks[b, padded - tail :, :] = jnp.zeros((tail, rows), jnp.bfloat16)
-        h_blocks[b, :depth, :] = hidden_vm[b * depth : (b + 1) * depth, :]
     together = 128 // math.gcd(padded, 128)
-    for b in range(0, n_roll, together):
-        turned = jnp.concatenate(
-            [h_blocks[block_of[b + n]] for n in range(together)], axis=0
-        ).T
-        h_all[:, b * padded : (b + together) * padded] = turned
-    if padded > depth:
+
+    def cut_hidden():
+        hidden_copy.wait()
         for b in range(n_roll):
-            w_phase[(b + 1) * padded - tail : (b + 1) * padded, :] = jnp.zeros(
-                (tail, w_phase.shape[1]), jnp.bfloat16
-            )
+            if padded > depth:
+                h_blocks[b, padded - tail :, :] = jnp.zeros((tail, rows), jnp.bfloat16)
+                w_phase[(b + 1) * padded - tail : (b + 1) * padded, :] = jnp.zeros(
+                    (tail, w_phase.shape[1]), jnp.bfloat16
+                )
+            h_blocks[b, :depth, :] = hidden_vm[b * depth : (b + 1) * depth, :]
+
+    def turn_hidden(first, count):
+        for b in range(first, first + count, together):
+            turned = jnp.concatenate(
+                [h_blocks[block_of[b + n]] for n in range(together)], axis=0
+            ).T
+            h_all[:, b * padded : (b + together) * padded] = turned
+
+    def key_angles():
+        cos_k[...] = jnp.cos(k_angle)
+        sin_k[...] = jnp.sin(k_angle)
 
     def project(phase):
+        if phase == 0:
+            sib_own(sibling).wait_recv()
+
+        def sib_step(step, carry):
+            for direction in range(2):
+                sib_copy(phase, direction, step, None, 1 - core).wait_recv()
+            return carry
+
+        lax.fori_loop(1, half_ring, sib_step, 0)
+        for direction in range(2):
+            sib_copy(phase, direction, half_ring, direction, 1 - core).wait_recv()
         first, count = phases[phase]
         for b in range(n_roll):
             for j in range(count):
@@ -365,59 +379,46 @@
         for i in range(1, n_seq):
             o_copy(i, h).start()
 
+    def wait_queries():
+        for i in range(1, n_seq):
+            for copy in q_copies(i, (seq - i + n_seq) % n_seq):
+                copy.wait_recv()
+
+    part = n_roll // 2
+    work = [
+        [
+            cut_hidden,
+            functools.partial(turn_hidden, 0, part),
+            functools.partial(turn_hidden, part, n_roll - part),
+            key_angles,
+        ]
+    ]
+    for first, count in phases:
+        work.append(
+            [functools.partial(project, len(work) - 1)]
+            + [functools.partial(one_head, first + j) for j in range(count)]
+        )
+    work[1].insert(1, wait_queries)
+
     for phase in range(len(phases)):
-        before, before_count = phases[phase - 1] if phase else (0, 0)
-        in_loop = min(before_count, half_ring - 1)
-
-        def step_body(step, carry):
+        items = list(work[phase])
+        for step in range(1, half_ring + 1):
+            whole = step < half_ring
             for direction in range(2):
-                ring_arrival(phase, direction, step, None).wait_recv()
-
-                @pl.when(step < half_ring - 1)
-                def _():
-                    ring_copy(phase, direction, step + 1, None).start()
-
-                @pl.when(step == half_ring - 1)
-                def _():
-                    ring_copy(phase, direction, step + 1, direction).start()
-
-                sib_copy(phase, direction, step, None, core).start()
-
-            if in_loop:
-
-                @pl.when(step <= in_loop)
-                def _():
-                    one_head(before + step - 1)
-
-            return carry
-
-        lax.fori_loop(1, half_ring, step_body, 0)
-        if phase + 2 < len(phases):
-            start_phase(phase + 2)
-        if phase == 0:
-            sib_own(sibling).wait_recv()
-            for i in range(1, n_seq):
-                for copy in q_copies(i, (seq - i + n_seq) % n_seq):
-                    copy.wait_recv()
-        for direction in range(2):
-            ring_arrival(phase, direction, half_ring, direction).wait_recv()
-            sib_copy(phase, direction, half_ring, direction, core).start()
-        for left_over in range(in_loop, before_count):
-            one_head(before + left_over)
-
-        def sib_step(step, carry):
-            for direction in range(2):
-                sib_copy(phase, direction, step, None, 1 - core).wait_recv()
-            return carry
-
-        lax.fori_loop(1, half_ring, sib_step, 0)
-        for direction in range(2):
-            sib_copy(phase, direction, half_ring, direction, 1 - core).wait_recv()
-        project(phase)
-
-    last, last_count = phases[-1]
-    for j in range(last_count):
-        one_head(last + j)
+                piece = None if whole else direction
+                ring_arrival(phase, direction, step, piece).wait_recv()
+                if whole:
+                    further = None if step + 1 < half_ring else direction
+                    ring_copy(phase, direction, step + 1, further).start()
+                sib_copy(phase, direction, step, piece, core).start()
+            if step == half_ring - 1 and phase + 2 < len(phases):
+                start_phase(phase + 2)
+            if items:
+                items.pop(0)()
+        for item in items:
+            item()
+    for item in work[-1]:
+        item()
     for i in range(1, n_seq):
         l_copy(i).start()
 
@@ -508,7 +509,7 @@
             pltpu.VMEM((model_width, rows), bf16),
             pltpu.VMEM((n_roll, padded, rows), bf16),
             pltpu.VMEM((rows, n_roll * padded), bf16),
-            pltpu.VMEM((n_roll * padded, columns // 2), bf16),
+            pltpu.VMEM((n_roll * padded, 256), bf16),
             pltpu.VMEM((rows, columns), f32),
             pltpu.VMEM((half, rows), f32),
             pltpu.VMEM((half, rows), f32),

time: 65.3 us -> 66.7 us (1.021)
  Pallas kernels: 63.4 us -> 64.9 us
    pallas_call x1, Pallas kernels: 63.4 us -> 64.9 us  [shards(): pl.pallas_call(functools.partial(kernel, n_roll, n_seq), out_shape=jax.Sh...]
where the time goes in v4:
time: 66.7 us; the launch traced here: 66.6 us
  Pallas kernels  64.9 us (97%)
  local copies, waits for them, and re-layouts  1.67 us (3%)
    pallas_call x1, Pallas kernels, shards(): pl.pallas_call(functools.partial(kernel, n_roll, n_seq), out_shape=jax.Sh...  64.9 us
    unnamed x1, local copies, waits for them, and re-layouts  1.67 us

profile of v4, /device:TPU:0, one launch (start us, length us, event | category | flops | bytes accessed | tf_op | source)
XLA Modules:
  0.0 66.6 jit_solution(10569973840303297557)
XLA Ops:
  0.0 64.9 %shard_map.73 = bf16[32,4096]{1,0:T(8,128)(2,1)} custom-call(s32[16]{0:T(128)} %block_of.1, bf16[180,1024]{1,0:T(8,128)(2,1)} %w_ref.1, bf16[2880,512]{1,0:T(8,128)(2,1)} %bitcast.6, bf16[32,4096]{1,0:T(8,128)(2,1)} %bitcast.7, s32[1,512]{1,0:T(1,128)} %key_pos_hbm.1, s32[1,32]{1,0:T(1,128)} %query_pos_hbm.1, f32[1,128]{1,0:T(1,128)} %constant.2.clone.freq_hbm), custom_call_target="tpu_custom_call" | custom-call | flops 3019898880 | bytes 2949120 | tf_op jit(solution)/shard_map/pallas_call | solution.py:490
  64.9 1.7 %copy.9 = bf16[1,32,4096]{2,1,0:T(8,128)(2,1)} copy(bf16[1,32,4096]{2,1,0:T(8,128)(2,1)} %bitcast.5) | data formatting | bytes 524288

commit v5 on v4

--- a/solution.py
+++ b/solution.py
@@ -385,24 +385,24 @@
                 copy.wait_recv()
 
     part = n_roll // 2
+    count = len(phases)
     work = [
-        [
-            cut_hidden,
-            functools.partial(turn_hidden, 0, part),
-            functools.partial(turn_hidden, part, n_roll - part),
-            key_angles,
-        ]
+        cut_hidden,
+        functools.partial(turn_hidden, 0, part),
+        functools.partial(turn_hidden, part, n_roll - part),
+        key_angles,
     ]
-    for first, count in phases:
-        work.append(
-            [functools.partial(project, len(work) - 1)]
-            + [functools.partial(one_head, first + j) for j in range(count)]
-        )
-    work[1].insert(1, wait_queries)
-
-    for phase in range(len(phases)):
-        items = list(work[phase])
-        for step in range(1, half_ring + 1):
+    later = [wait_queries]
+    for phase in range(count):
+        later.append(functools.partial(project, phase))
+        first, many = phases[phase]
+        later += [functools.partial(one_head, first + j) for j in range(many)]
+
+    for tick in range(1, half_ring + count):
+        for phase in range(count):
+            step = tick - phase
+            if not 1 <= step <= half_ring:
+                continue
             whole = step < half_ring
             for direction in range(2):
                 piece = None if whole else direction
@@ -411,13 +411,14 @@
                     further = None if step + 1 < half_ring else direction
                     ring_copy(phase, direction, step + 1, further).start()
                 sib_copy(phase, direction, step, piece, core).start()
-            if step == half_ring - 1 and phase + 2 < len(phases):
-                start_phase(phase + 2)
-            if items:
-                items.pop(0)()
-        for item in items:
-            item()
-    for item in work[-1]:
+        if 2 <= tick + 1 < count:
+            start_phase(tick + 1)
+        if work:
+            work.pop(0)()
+        elif tick > half_ring:
+            for _ in range(2):
+                later.pop(0)()
+    for item in later:
         item()
     for i in range(1, n_seq):
         l_copy(i).start()

time: 66.7 us -> 59.9 us (0.90)
  Pallas kernels: 64.9 us -> 58 us
    pallas_call x1, Pallas kernels: 64.9 us -> 58 us  [shards(): pl.pallas_call(functools.partial(kernel, n_roll, n_seq), out_shape=jax.Sh...]
where the time goes in v5:
time: 59.9 us; the launch traced here: 59.7 us
  Pallas kernels  58 us (97%)
  local copies, waits for them, and re-layouts  1.67 us (3%)
    pallas_call x1, Pallas kernels, shards(): pl.pallas_call(functools.partial(kernel, n_roll, n_seq), out_shape=jax.Sh...  58 us
    unnamed x1, local copies, waits for them, and re-layouts  1.67 us

profile of v5, /device:TPU:0, one launch (start us, length us, event | category | flops | bytes accessed | tf_op | source)
XLA Modules:
  0.0 59.7 jit_solution(15900967956737725224)
XLA Ops:
  0.0 58.0 %shard_map.73 = bf16[32,4096]{1,0:T(8,128)(2,1)} custom-call(s32[16]{0:T(128)} %block_of.1, bf16[180,1024]{1,0:T(8,128)(2,1)} %w_ref.1, bf16[2880,512]{1,0:T(8,128)(2,1)} %bitcast.6, bf16[32,4096]{1,0:T(8,128)(2,1)} %bitcast.7, s32[1,512]{1,0:T(1,128)} %key_pos_hbm.1, s32[1,32]{1,0:T(1,128)} %query_pos_hbm.1, f32[1,128]{1,0:T(1,128)} %constant.2.clone.freq_hbm), custom_call_target="tpu_custom_call" | custom-call | flops 3019898880 | bytes 2949120 | tf_op jit(solution)/shard_map/pallas_call | solution.py:491
  58.0 1.7 %copy.9 = bf16[1,32,4096]{2,1,0:T(8,128)(2,1)} copy(bf16[1,32,4096]{2,1,0:T(8,128)(2,1)} %bitcast.5) | data formatting | bytes 524288
